TPU v7x, 256 devices: a whole 4x4x8 slice. The times are simulated.
256 devices in a mesh: ctx: 32 (over y_lo, z, core), head: 8 (over y_hi, x).
Axes of the slice: x: 4, y: 4 (y_hi: 2, y_lo: 2; y = y_hi * 2 + y_lo), z: 8, core: 2. Of those that a mesh axis runs over, the one named last changes fastest.
Arguments:
- queries: bfloat16 [32768, 1024], P(('ctx', 'head')), may hold values from -15 to 15
- keys: bfloat16 [32768, 128], P(('ctx', 'head')), may hold values from -12 to 12
- values: bfloat16 [32768, 128], P(('ctx', 'head')), may hold values from -6 to 6
- doc_lengths: int32 [16], replicated, may hold values from 1 to 17408, 32768 in all
Outputs:
- attended: bfloat16 [32768, 1024], P(('ctx', 'head'))
Inputs may be any that keep to these rules, and one draw needn't show every extreme that they name: `doc_lengths`: the 16 lengths sum to 32768 and the largest is 17408.
All inputs are finite; a program needn't handle non-finite values.
Results may differ from a plain program's by a relative error of at most 0.0049.
Values may be sent and summed in bfloat16 or wider, within the bound.
A program may use at most 64 MiB of HBM per device.

v0:
```python
import math

import jax
import jax.numpy as jnp
from jax import lax
from jax.sharding import PartitionSpec as P


def doc_starts(lengths, positions):
    ends = jnp.cumsum(lengths)
    chosen = jnp.where(ends[None, :] <= positions[:, None], lengths[None, :], 0)
    return jnp.sum(chosen, axis=1)


def per_device(queries, keys, values, doc_lengths):
    head_dim = keys.shape[1]
    factor = 1.0 / (30.0 * math.sqrt(head_dim))
    query_rows = lax.all_to_all(queries, "head", split_axis=1, concat_axis=0, tiled=True)
    first_pos = lax.axis_index("ctx") * query_rows.shape[0]
    row_count = query_rows.shape[0]
    heads_here = query_rows.shape[1] // head_dim
    query_pos = first_pos + jnp.arange(row_count, dtype=jnp.int32)
    starts = doc_starts(doc_lengths, query_pos)
    row_pos = jnp.repeat(query_pos, heads_here)
    row_start = jnp.repeat(starts, heads_here)
    last_pos = first_pos + row_count - 1
    earliest = starts[0]
    initial = (
        jnp.zeros((row_count * heads_here, head_dim), jnp.float32),
        jnp.zeros((row_count * heads_here,), jnp.float32),
    )
    shard_keys, shard_values = (
        lax.all_gather(keys, "head", axis=0, tiled=True),
        lax.all_gather(values, "head", axis=0, tiled=True),
    )
    key_piece = lax.all_gather(shard_keys, "ctx", axis=0, tiled=True)
    value_piece = lax.all_gather(shard_values, "ctx", axis=0, tiled=True)
    length = key_piece.shape[0]
    block_len = math.gcd(length, 1024)
    block_count = length // block_len

    def one_block(block_index, totals):
        offset = block_index * block_len

        def compute(current):
            key_block = lax.dynamic_slice_in_dim(key_piece, offset, block_len, 0)
            value_block = lax.dynamic_slice_in_dim(value_piece, offset, block_len, 0)
            scores = lax.dot_general(
                query_rows, key_block, (((1,), (1,)), ((), ())), preferred_element_type=jnp.float32
            )
            capped = 30.0 * jnp.tanh(scores * factor)
            key_pos = offset + jnp.arange(block_len, dtype=jnp.int32)
            allowed = (key_pos[None, :] <= row_pos[:, None]) & (
                key_pos[None, :] >= row_start[:, None]
            )
            weights = jnp.where(allowed, jnp.exp(capped), jnp.float32(0.0))
            added = jnp.dot(
                weights.astype(jnp.bfloat16), value_block, preferred_element_type=jnp.float32
            )
            return (current[0] + added, current[1] + jnp.sum(weights, axis=1))

        needed = (offset <= last_pos) & (offset + block_len - 1 >= earliest)
        return lax.cond(needed, compute, lambda current: current, totals)

    numerator, denominator = lax.fori_loop(0, block_count, one_block, initial)
    output = (numerator / denominator[:, None]).astype(jnp.bfloat16)
    return lax.all_to_all(output, "head", split_axis=0, concat_axis=1, tiled=True)


def solution(mesh):
    return jax.shard_map(
        per_device,
        mesh=mesh,
        in_specs=(
            P(("ctx", "head"), None),
            P(("ctx", "head"), None),
            P(("ctx", "head"), None),
            P(),
        ),
        out_specs=P(("ctx", "head"), None),
        check_vma=False,
    )
```

profile of v0, /device:TPU:168, one launch (start us, length us, event | category | flops | bytes accessed | tf_op | source)
XLA Modules:
  0.0 327.4 jit_solution(6778996393014405219)
XLA Ops:
  6.5 36.9 %all_gather.12 = bf16[1024,128]{1,0:T(8,128)(2,1)} all-gather(bf16[128,128]{1,0:T(8,128)(2,1)} %param.9), channel_id=1, replica_groups=mesh['ctx'=32,'head'=8] {'head'}, dimensions={0}, use_global_device_ids=true | all-gather | bytes 294912 | tf_op jit(solution)/shard_map/all_gather | solution.py:33
  43.5 36.6 %all_gather.14 = bf16[1024,128]{1,0:T(8,128)(2,1)} all-gather(bf16[128,128]{1,0:T(8,128)(2,1)} %param.10), channel_id=1, replica_groups=mesh['ctx'=32,'head'=8] {'head'}, dimensions={0}, use_global_device_ids=true | all-gather | bytes 294912 | tf_op jit(solution)/shard_map/all_gather | solution.py:34
  80.9 5.6 %all-to-all-start = ((bf16[128,8,128]{2,0,1:T(8,128)(2,1)}), bf16[128,8,128]{2,0,1:T(8,128)(2,1)S(1)}, u32[]{:S(2)}, u32[]{:S(2)}) async-start(bf16[128,8,128]{2,0,1:T(8,128)(2,1)} %copy_bitcast_fusion), calls=%async_computation | async-start | bytes 524288 | tf_op jit(solution)/shard_map/all_to_all | solution.py:18
  88.7 6.6 %all-to-all-done = bf16[128,8,128]{2,0,1:T(8,128)(2,1)S(1)} async-done(((bf16[128,8,128]{2,0,1:T(8,128)(2,1)}), bf16[128,8,128]{2,0,1:T(8,128)(2,1)S(1)}, u32[]{:S(2)}, u32[]{:S(2)}) %all-to-all-start) | async-done | bytes 262176 | tf_op jit(solution)/shard_map/all_to_all | solution.py:18
  95.3 18.6 %all-gather.3.cloned.1.call-done = bf16[32768,128]{1,0:T(8,128)(2,1)} async-done(((bf16[1024,128]{1,0:T(8,128)(2,1)}), bf16[32768,128]{1,0:T(8,128)(2,1)}) %all-gather.3.cloned.1.call-update) | async-done | bytes 8388624 | tf_op jit(solution)/shard_map/all_gather | solution.py:36
  114.0 74.3 %all-gather.5.cloned.1.call-done = bf16[32768,128]{1,0:T(8,128)(2,1)} async-done(((bf16[1024,128]{1,0:T(8,128)(2,1)}), bf16[32768,128]{1,0:T(8,128)(2,1)}) %all-gather.5.cloned.1.call-update) | async-done | bytes 8388624 | tf_op jit(solution)/shard_map/all_gather | solution.py:37
  188.3 116.5 %while.20 = (s32[]{:T(128)}, f32[1024,128]{1,0:T(8,128)S(1)}, f32[1024]{0:T(1024)S(1)}, s32[]{:T(128)}, s32[]{:T(128)}, /*index=5*/s32[1024]{0:T(1024)S(1)}, bf1...) while((s32[]{:T(128)}, f32[1024,128]{1,0:T(8,128)S(1)}, ...), condition=%wide.region_6.7_spmd.clone, body=%wide.region_2.6_spmd.clone.sunk | while | flops 551684096 | bytes 10281297 | solution.py:65
  194.5 5.4 %conditional.3 = ((f32[1024,128]{1,0:T(8,128)S(1)}, f32[1024]{0:T(1024)S(1)})) conditional(s32[]{:T(128)} %convert_element_type.27, (f32[1024,128]{1,0:T(8,128)S(1)}, f32[1024]{0:T(1024)S(1)}) %tuple.60, (s32[]{:T(128)}, s32[]{:T(128)}, s32[1024]{0:T(1024)S(1)}, bf16[32768,128]{1,0:T(8,128)(2,1)}, bf16[1024,128]{1,0:T(8,128)(2,1)S(1)}, ...), branch_computations={%region_3.3_spmd, %region_4.5_spmd} | conditional | flops 551684096 | bytes 10276938 | solution.py:63
  194.6 2.7 fusion.2
  200.5 5.4 %conditional.3 = ((f32[1024,128]{1,0:T(8,128)S(1)}, f32[1024]{0:T(1024)S(1)})) conditional(s32[]{:T(128)} %convert_element_type.27, (f32[1024,128]{1,0:T(8,128)S(1)}, f32[1024]{0:T(1024)S(1)}) %tuple.60, (s32[]{:T(128)}, s32[]{:T(128)}, s32[1024]{0:T(1024)S(1)}, bf16[32768,128]{1,0:T(8,128)(2,1)}, bf16[1024,128]{1,0:T(8,128)(2,1)S(1)}, ...), branch_computations={%region_3.3_spmd, %region_4.5_spmd} | conditional | flops 551684096 | bytes 10276938 | solution.py:63
  200.6 2.7 fusion.2
  206.5 5.4 %conditional.3 = ((f32[1024,128]{1,0:T(8,128)S(1)}, f32[1024]{0:T(1024)S(1)})) conditional(s32[]{:T(128)} %convert_element_type.27, (f32[1024,128]{1,0:T(8,128)S(1)}, f32[1024]{0:T(1024)S(1)}) %tuple.60, (s32[]{:T(128)}, s32[]{:T(128)}, s32[1024]{0:T(1024)S(1)}, bf16[32768,128]{1,0:T(8,128)(2,1)}, bf16[1024,128]{1,0:T(8,128)(2,1)S(1)}, ...), branch_computations={%region_3.3_spmd, %region_4.5_spmd} | conditional | flops 551684096 | bytes 10276938 | solution.py:63
  212.5 5.4 %conditional.3 = ((f32[1024,128]{1,0:T(8,128)S(1)}, f32[1024]{0:T(1024)S(1)})) conditional(s32[]{:T(128)} %convert_element_type.27, (f32[1024,128]{1,0:T(8,128)S(1)}, f32[1024]{0:T(1024)S(1)}) %tuple.60, (s32[]{:T(128)}, s32[]{:T(128)}, s32[1024]{0:T(1024)S(1)}, bf16[32768,128]{1,0:T(8,128)(2,1)}, bf16[1024,128]{1,0:T(8,128)(2,1)S(1)}, ...), branch_computations={%region_3.3_spmd, %region_4.5_spmd} | conditional | flops 551684096 | bytes 10276938 | solution.py:63
  218.5 5.4 %conditional.3 = ((f32[1024,128]{1,0:T(8,128)S(1)}, f32[1024]{0:T(1024)S(1)})) conditional(s32[]{:T(128)} %convert_element_type.27, (f32[1024,128]{1,0:T(8,128)S(1)}, f32[1024]{0:T(1024)S(1)}) %tuple.60, (s32[]{:T(128)}, s32[]{:T(128)}, s32[1024]{0:T(1024)S(1)}, bf16[32768,128]{1,0:T(8,128)(2,1)}, bf16[1024,128]{1,0:T(8,128)(2,1)S(1)}, ...), branch_computations={%region_3.3_spmd, %region_4.5_spmd} | conditional | flops 551684096 | bytes 10276938 | solution.py:63
  218.5 2.7 fusion.2
  224.5 5.4 %conditional.3 = ((f32[1024,128]{1,0:T(8,128)S(1)}, f32[1024]{0:T(1024)S(1)})) conditional(s32[]{:T(128)} %convert_element_type.27, (f32[1024,128]{1,0:T(8,128)S(1)}, f32[1024]{0:T(1024)S(1)}) %tuple.60, (s32[]{:T(128)}, s32[]{:T(128)}, s32[1024]{0:T(1024)S(1)}, bf16[32768,128]{1,0:T(8,128)(2,1)}, bf16[1024,128]{1,0:T(8,128)(2,1)S(1)}, ...), branch_computations={%region_3.3_spmd, %region_4.5_spmd} | conditional | flops 551684096 | bytes 10276938 | solution.py:63
  230.5 5.4 %conditional.3 = ((f32[1024,128]{1,0:T(8,128)S(1)}, f32[1024]{0:T(1024)S(1)})) conditional(s32[]{:T(128)} %convert_element_type.27, (f32[1024,128]{1,0:T(8,128)S(1)}, f32[1024]{0:T(1024)S(1)}) %tuple.60, (s32[]{:T(128)}, s32[]{:T(128)}, s32[1024]{0:T(1024)S(1)}, bf16[32768,128]{1,0:T(8,128)(2,1)}, bf16[1024,128]{1,0:T(8,128)(2,1)S(1)}, ...), branch_computations={%region_3.3_spmd, %region_4.5_spmd} | conditional | flops 551684096 | bytes 10276938 | solution.py:63
  236.5 5.4 %conditional.3 = ((f32[1024,128]{1,0:T(8,128)S(1)}, f32[1024]{0:T(1024)S(1)})) conditional(s32[]{:T(128)} %convert_element_type.27, (f32[1024,128]{1,0:T(8,128)S(1)}, f32[1024]{0:T(1024)S(1)}) %tuple.60, (s32[]{:T(128)}, s32[]{:T(128)}, s32[1024]{0:T(1024)S(1)}, bf16[32768,128]{1,0:T(8,128)(2,1)}, bf16[1024,128]{1,0:T(8,128)(2,1)S(1)}, ...), branch_computations={%region_3.3_spmd, %region_4.5_spmd} | conditional | flops 551684096 | bytes 10276938 | solution.py:63
  236.5 2.7 fusion.2
  242.4 5.4 %conditional.3 = ((f32[1024,128]{1,0:T(8,128)S(1)}, f32[1024]{0:T(1024)S(1)})) conditional(s32[]{:T(128)} %convert_element_type.27, (f32[1024,128]{1,0:T(8,128)S(1)}, f32[1024]{0:T(1024)S(1)}) %tuple.60, (s32[]{:T(128)}, s32[]{:T(128)}, s32[1024]{0:T(1024)S(1)}, bf16[32768,128]{1,0:T(8,128)(2,1)}, bf16[1024,128]{1,0:T(8,128)(2,1)S(1)}, ...), branch_computations={%region_3.3_spmd, %region_4.5_spmd} | conditional | flops 551684096 | bytes 10276938 | solution.py:63
  248.4 5.4 %conditional.3 = ((f32[1024,128]{1,0:T(8,128)S(1)}, f32[1024]{0:T(1024)S(1)})) conditional(s32[]{:T(128)} %convert_element_type.27, (f32[1024,128]{1,0:T(8,128)S(1)}, f32[1024]{0:T(1024)S(1)}) %tuple.60, (s32[]{:T(128)}, s32[]{:T(128)}, s32[1024]{0:T(1024)S(1)}, bf16[32768,128]{1,0:T(8,128)(2,1)}, bf16[1024,128]{1,0:T(8,128)(2,1)S(1)}, ...), branch_computations={%region_3.3_spmd, %region_4.5_spmd} | conditional | flops 551684096 | bytes 10276938 | solution.py:63
  254.4 5.4 %conditional.3 = ((f32[1024,128]{1,0:T(8,128)S(1)}, f32[1024]{0:T(1024)S(1)})) conditional(s32[]{:T(128)} %convert_element_type.27, (f32[1024,128]{1,0:T(8,128)S(1)}, f32[1024]{0:T(1024)S(1)}) %tuple.60, (s32[]{:T(128)}, s32[]{:T(128)}, s32[1024]{0:T(1024)S(1)}, bf16[32768,128]{1,0:T(8,128)(2,1)}, bf16[1024,128]{1,0:T(8,128)(2,1)S(1)}, ...), branch_computations={%region_3.3_spmd, %region_4.5_spmd} | conditional | flops 551684096 | bytes 10276938 | solution.py:63
  254.5 2.7 fusion.2
  260.4 5.4 %conditional.3 = ((f32[1024,128]{1,0:T(8,128)S(1)}, f32[1024]{0:T(1024)S(1)})) conditional(s32[]{:T(128)} %convert_element_type.27, (f32[1024,128]{1,0:T(8,128)S(1)}, f32[1024]{0:T(1024)S(1)}) %tuple.60, (s32[]{:T(128)}, s32[]{:T(128)}, s32[1024]{0:T(1024)S(1)}, bf16[32768,128]{1,0:T(8,128)(2,1)}, bf16[1024,128]{1,0:T(8,128)(2,1)S(1)}, ...), branch_computations={%region_3.3_spmd, %region_4.5_spmd} | conditional | flops 551684096 | bytes 10276938 | solution.py:63
  266.4 5.4 %conditional.3 = ((f32[1024,128]{1,0:T(8,128)S(1)}, f32[1024]{0:T(1024)S(1)})) conditional(s32[]{:T(128)} %convert_element_type.27, (f32[1024,128]{1,0:T(8,128)S(1)}, f32[1024]{0:T(1024)S(1)}) %tuple.60, (s32[]{:T(128)}, s32[]{:T(128)}, s32[1024]{0:T(1024)S(1)}, bf16[32768,128]{1,0:T(8,128)(2,1)}, bf16[1024,128]{1,0:T(8,128)(2,1)S(1)}, ...), branch_computations={%region_3.3_spmd, %region_4.5_spmd} | conditional | flops 551684096 | bytes 10276938 | solution.py:63
  272.4 5.4 %conditional.3 = ((f32[1024,128]{1,0:T(8,128)S(1)}, f32[1024]{0:T(1024)S(1)})) conditional(s32[]{:T(128)} %convert_element_type.27, (f32[1024,128]{1,0:T(8,128)S(1)}, f32[1024]{0:T(1024)S(1)}) %tuple.60, (s32[]{:T(128)}, s32[]{:T(128)}, s32[1024]{0:T(1024)S(1)}, bf16[32768,128]{1,0:T(8,128)(2,1)}, bf16[1024,128]{1,0:T(8,128)(2,1)S(1)}, ...), branch_computations={%region_3.3_spmd, %region_4.5_spmd} | conditional | flops 551684096 | bytes 10276938 | solution.py:63
  278.4 5.4 %conditional.3 = ((f32[1024,128]{1,0:T(8,128)S(1)}, f32[1024]{0:T(1024)S(1)})) conditional(s32[]{:T(128)} %convert_element_type.27, (f32[1024,128]{1,0:T(8,128)S(1)}, f32[1024]{0:T(1024)S(1)}) %tuple.60, (s32[]{:T(128)}, s32[]{:T(128)}, s32[1024]{0:T(1024)S(1)}, bf16[32768,128]{1,0:T(8,128)(2,1)}, bf16[1024,128]{1,0:T(8,128)(2,1)S(1)}, ...), branch_computations={%region_3.3_spmd, %region_4.5_spmd} | conditional | flops 551684096 | bytes 10276938 | solution.py:63
  284.4 5.4 %conditional.3 = ((f32[1024,128]{1,0:T(8,128)S(1)}, f32[1024]{0:T(1024)S(1)})) conditional(s32[]{:T(128)} %convert_element_type.27, (f32[1024,128]{1,0:T(8,128)S(1)}, f32[1024]{0:T(1024)S(1)}) %tuple.60, (s32[]{:T(128)}, s32[]{:T(128)}, s32[1024]{0:T(1024)S(1)}, bf16[32768,128]{1,0:T(8,128)(2,1)}, bf16[1024,128]{1,0:T(8,128)(2,1)S(1)}, ...), branch_computations={%region_3.3_spmd, %region_4.5_spmd} | conditional | flops 551684096 | bytes 10276938 | solution.py:63
  290.3 5.4 %conditional.3 = ((f32[1024,128]{1,0:T(8,128)S(1)}, f32[1024]{0:T(1024)S(1)})) conditional(s32[]{:T(128)} %convert_element_type.27, (f32[1024,128]{1,0:T(8,128)S(1)}, f32[1024]{0:T(1024)S(1)}) %tuple.60, (s32[]{:T(128)}, s32[]{:T(128)}, s32[1024]{0:T(1024)S(1)}, bf16[32768,128]{1,0:T(8,128)(2,1)}, bf16[1024,128]{1,0:T(8,128)(2,1)S(1)}, ...), branch_computations={%region_3.3_spmd, %region_4.5_spmd} | conditional | flops 551684096 | bytes 10276938 | solution.py:63
  290.4 2.7 fusion.2
  296.3 5.4 %conditional.3 = ((f32[1024,128]{1,0:T(8,128)S(1)}, f32[1024]{0:T(1024)S(1)})) conditional(s32[]{:T(128)} %convert_element_type.27, (f32[1024,128]{1,0:T(8,128)S(1)}, f32[1024]{0:T(1024)S(1)}) %tuple.60, (s32[]{:T(128)}, s32[]{:T(128)}, s32[1024]{0:T(1024)S(1)}, bf16[32768,128]{1,0:T(8,128)(2,1)}, bf16[1024,128]{1,0:T(8,128)(2,1)S(1)}, ...), branch_computations={%region_3.3_spmd, %region_4.5_spmd} | conditional | flops 551684096 | bytes 10276938 | solution.py:63
  305.1 14.5 %all_to_all.38 = bf16[8,128,128]{2,1,0:T(8,128)(2,1)S(1)} all-to-all(bf16[8,128,128]{2,1,0:T(8,128)(2,1)S(1)} %bitcast.24), channel_id=1, replica_groups=mesh['ctx'=32,'head'=8] {'head'}, dimensions={0} | all-to-all | bytes 524288 | tf_op jit(solution)/shard_map/all_to_all | solution.py:67
  (130 shorter events, 84.3 us)
Async XLA Ops:
  6.5 73.6 %copy-start = (bf16[128,1024]{1,0:T(8,128)(2,1)S(1)}, bf16[128,1024]{1,0:T(8,128)(2,1)}, u32[]{:S(2)}) copy-start(bf16[128,1024]{1,0:T(8,128)(2,1)} %param.8) | copy-start | bytes 786436
  6.5 107.4 %all-gather.3.cloned.1.call-start = ((), (), s32[]{:S(2)}) async-start(), calls=%async_computation.2 | async-start | bytes 8650752 | tf_op jit(solution)/shard_map/all_gather | solution.py:36
  43.4 144.8 %all-gather.5.cloned.1.call-start = ((), (), s32[]{:S(2)}) async-start(), calls=%async_computation.3 | async-start | bytes 8650752 | tf_op jit(solution)/shard_map/all_gather | solution.py:37
  80.9 14.4 %all-to-all-start = ((bf16[128,8,128]{2,0,1:T(8,128)(2,1)}), bf16[128,8,128]{2,0,1:T(8,128)(2,1)S(1)}, u32[]{:S(2)}, u32[]{:S(2)}) async-start(bf16[128,8,128]{2,0,1:T(8,128)(2,1)} %copy_bitcast_fusion), calls=%async_computation | async-start | bytes 524288 | tf_op jit(solution)/shard_map/all_to_all | solution.py:18
Sparse Core Ops, SparseCore 0:
  43.6 70.3 all-gather.2
  115.8 72.4 all-gather.4
where the time goes:
time: 329 us; the launch traced here: 327 us
  waiting for transfers between devices  99.6 us (30%)
  matrix products  95.7 us (29%)
  blocking collectives  88 us (27%)
  loops' own time  20.5 us (6%)
  between operations  13.4 us (4%)
  starting transfers between devices  5.69 us (2%)
    all_gather x1, waiting for transfers between devices, per_device(): value_piece = lax.all_gather(shard_values, 'ctx', axis=0, tiled=True)  74.3 us
    dot_general x18, matrix products, compute(): lax.dot_general(query_rows, key_block, (((1,), (1,)), ((), ())), preferre...  48.4 us
    dot_general x18, matrix products, compute(): jnp.dot(weights.astype(jnp.bfloat16), value_block, preferred_element_type...  47.3 us
    all_gather x1, blocking collectives, per_device(): lax.all_gather(keys, 'head', axis=0, tiled=True)  36.9 us
    all_gather x1, blocking collectives, per_device(): lax.all_gather(values, 'head', axis=0, tiled=True)  36.6 us
    another operation x1, loops' own time, per_device(): numerator, denominator = lax.fori_loop(0, block_count, one_block, initial)  19.4 us
    all_gather x1, waiting for transfers between devices, per_device(): key_piece = lax.all_gather(shard_keys, 'ctx', axis=0, tiled=True)  18.6 us
    all_to_all x1, blocking collectives, per_device(): lax.all_to_all(output, 'head', split_axis=0, concat_axis=1, tiled=True)  14.5 us
  transfers between devices with their start and end apart: 3, of which 3 were waited for; matrix products, arithmetic and copies ran while one was open for 1% of the time, Pallas kernels for 0%

commit v1 on v0

v1 whole, which is shorter than its diff:
```python
import functools
import math

import jax
import jax.numpy as jnp
from jax import lax
from jax.experimental import pallas as pl
from jax.experimental.pallas import tpu as pltpu
from jax.sharding import PartitionSpec as P

MESH = pl.DeviceIdType.MESH
HD = 128
HEADS = 8
TOK = 128
NDOCS = 16
ROWS = HEADS * TOK
FACTOR = 1.0 / (30.0 * math.sqrt(HD))
GAIN = 30.0 * math.log2(math.e)
PAD = 4
LAST = 34
SLOTS = PAD + LAST + 2


def rows_of(slot, count=1):
    first = (slot + PAD) * TOK
    if not isinstance(first, int):
        first = pl.multiple_of(first, TOK)
    return pl.ds(first, count * TOK)


def kernel(
    q_ref, k_ref, v_ref, len_ref, o_ref,
    kv, qbuf, starts, acc, osend, orecv, dsend, drecv,
    kv_recv, kv_send, q_recv, q_send, o_recv, o_send, d_recv, d_send,
):
    ctx = lax.axis_index("ctx")
    head = lax.axis_index("head")
    L = ctx // 2
    c = ctx % 2
    h = head // 4
    x = head % 4
    w = 2 * c + h
    u = 4 * L + w

    chain_next = (ctx + 2, head)
    chain_prev = (ctx - 2, head)
    yh_peer = (ctx, (1 - h) * 4 + x)
    sib_peer = (L * 2 + 1 - c, head)

    def x_peer(j):
        return (ctx, h * 4 + (x + j) % 4)

    kv[...] = jnp.zeros_like(kv)
    kv[rows_of(LAST), 0:HD] = k_ref[...]
    kv[rows_of(LAST), HD:] = v_ref[...]
    for a in range(HEADS):
        qbuf[0, a * TOK:(a + 1) * TOK, :] = q_ref[:, a * HD:(a + 1) * HD]

    barrier = pltpu.get_barrier_semaphore()
    for peer in (yh_peer, sib_peer, x_peer(1), x_peer(2), x_peer(3)):
        pl.semaphore_signal(barrier, inc=1, device_id=peer, device_id_type=MESH)

    @pl.when(L < 15)
    def _():
        pl.semaphore_signal(barrier, inc=1, device_id=chain_next, device_id_type=MESH)

    @pl.when(L > 0)
    def _():
        pl.semaphore_signal(barrier, inc=1, device_id=chain_prev, device_id_type=MESH)

    for j in range(4):
        pos = (4 * u + (x + j) % 4) * TOK + lax.broadcasted_iota(jnp.int32, (TOK, TOK), 0)
        end = jnp.int32(0)
        start = jnp.zeros((TOK, TOK), jnp.int32)
        for d in range(NDOCS):
            length = len_ref[d]
            end = end + length
            start = start + jnp.where(pos >= end, length, 0)
        starts[j] = start

    pl.semaphore_wait(barrier, 5 + (L < 15).astype(jnp.int32) + (L > 0).astype(jnp.int32))

    def q_copy(j):
        return pltpu.make_async_remote_copy(
            src_ref=qbuf.at[0], dst_ref=qbuf.at[j], send_sem=q_send.at[j - 1],
            recv_sem=q_recv.at[j - 1], device_id=x_peer(4 - j), device_id_type=MESH)

    def o_copy(j):
        return pltpu.make_async_remote_copy(
            src_ref=osend.at[j - 1], dst_ref=orecv.at[j - 1], send_sem=o_send.at[j - 1],
            recv_sem=o_recv.at[j - 1], device_id=x_peer(j), device_id_type=MESH)

    def d_copy(j):
        return pltpu.make_async_remote_copy(
            src_ref=dsend.at[j - 1], dst_ref=drecv.at[j - 1], send_sem=d_send.at[j - 1],
            recv_sem=d_recv.at[j - 1], device_id=x_peer(j), device_id_type=MESH)

    def kv_copy(src, dst, kind, k, peer):
        return pltpu.make_async_remote_copy(
            src_ref=kv.at[rows_of(src)], dst_ref=kv.at[rows_of(dst)], send_sem=kv_send.at[kind, k],
            recv_sem=kv_recv.at[dst + PAD], device_id=peer, device_id_type=MESH)

    def chain_ok(k):
        if k == 0 or k > 9:
            return None
        ok = L >= k
        return ok if k <= 8 else ok & (c == 1)

    def chain_send_ok(k):
        ok = (L >= k) & (L < 15)
        if k + 1 <= 8:
            return ok
        return ok & (c == 1) if k + 1 == 9 else None

    def yh_ok(k, to_h):
        ok = L >= k
        if k == 0:
            return ok & ~((c == 1) & (to_h == 0))
        if k == 9:
            return ok & (c == 1) & (to_h == 0)
        return ok

    def sib_ok(k, to_c):
        ok = L >= k
        if k == 0:
            return ok & (to_c == 1)
        if k == 9:
            return ok & (to_c == 0)
        return ok

    def diag_ok(k, to_c):
        ok = L >= k
        if k == 0:
            return ok & (to_c == 1)
        if k == 8:
            return ok & ~((to_c == 1) & (h == 1))
        if k == 9:
            return ok & (to_c == 0) & (h == 0)
        return ok

    def chain_out(k):
        return kv_copy(LAST - 4 * k, LAST - 4 * (k + 1), 0, k, chain_next)

    def yh_out(k):
        return kv_copy(LAST - 4 * k, LAST - 4 * k + 2 * h - 1, 1, k, yh_peer)

    def sib_out(k):
        return kv_copy(LAST - 4 * k, LAST - 4 * k + 4 * c - 2, 2, k, sib_peer)

    def diag_out(k):
        return kv_copy(LAST - 4 * k + 1 - 2 * h, LAST - 4 * k + 4 * c - 1 - 2 * h, 3, k, sib_peer)

    def arrived(slot):
        kv_copy(slot, slot, 0, 0, sib_peer).wait_recv()

    def when(cond, body):
        if cond is not None:
            pl.when(cond)(body)

    def step_chain(k):
        when(chain_ok(k), lambda: arrived(LAST - 4 * k))
        when(chain_send_ok(k), lambda: chain_out(k).start())
        has = L >= k if k <= 8 else (L >= k) & (c == 1)
        when(has & yh_ok(k, 1 - h), lambda: yh_out(k).start())
        when(has & sib_ok(k, 1 - c), lambda: sib_out(k).start())

    def step_yh(k):
        when(yh_ok(k, h), lambda: arrived(LAST - 4 * k + 1 - 2 * h))
        when(diag_ok(k, 1 - c), lambda: diag_out(k).start())

    def step_sib(k):
        when(sib_ok(k, c), lambda: arrived(LAST - 4 * k + 2 - 4 * c))
        when(diag_ok(k, c), lambda: arrived(LAST - 4 * k + 3 - 4 * c - 2 * h))

    lane = lax.broadcasted_iota(jnp.int32, (TOK, TOK), 1)
    sub = lax.broadcasted_iota(jnp.int32, (TOK, TOK), 0)
    eye = lane == sub

    def part(j, a, first, count):
        q = qbuf[j, pl.ds(a * TOK, TOK), :]
        k = kv[rows_of(first, count), 0:HD]
        v = kv[rows_of(first, count), HD:]
        v = jnp.concatenate([v, jnp.ones_like(v)], axis=1)
        s = lax.dot_general(q, k, (((1,), (1,)), ((), ())), preferred_element_type=jnp.float32)
        p = jnp.exp2(jnp.tanh(s * FACTOR) * GAIN)
        start = starts[j]
        tiles = []
        for t in range(count):
            slot = first + t
            key_pos = (4 * (u - LAST + slot) + x) * TOK + lane
            ok = key_pos >= start
            if slot == LAST:
                ok = ok & (key_pos <= (4 * u + (x + j) % 4) * TOK + sub)
            tiles.append(jnp.where(ok, p[:, t * TOK:(t + 1) * TOK], 0.0).astype(jnp.bfloat16))
        return jnp.dot(jnp.concatenate(tiles, axis=1), v, preferred_element_type=jnp.float32)

    def add(j, first, count, fresh=False):
        def one(a, carry):
            rows = pl.ds(a * TOK, TOK)
            new = part(j, a, first, count)
            acc[j, rows, :] = new if fresh else acc[j, rows, :] + new
            return carry
        lax.fori_loop(0, HEADS, one, 0)

    def give(j, total_of):
        def one(a, carry):
            total = total_of(a)
            osend[j - 1, pl.ds(a * TOK, TOK), :] = total[:, 0:HD].astype(jnp.bfloat16)
            dsend[j - 1, pl.ds(a, 1), :] = jnp.sum(jnp.where(eye, total[:, HD:], 0.0), axis=0, keepdims=True)
            return carry
        lax.fori_loop(0, HEADS, one, 0)
        o_copy(j).start()
        d_copy(j).start()

    R0, R1, R2, R3, R4 = (31, 4), (23, 8), (15, 8), (7, 8), (0, 7)

    step_chain(0)
    q_copy(1).start()
    q_copy(3).start()
    step_yh(0); step_chain(1); step_sib(0); step_yh(1); step_chain(2); step_sib(1)
    add(0, *R0, fresh=True)
    q_copy(2).start()
    step_yh(2); step_chain(3); step_sib(2); step_yh(3); step_chain(4); step_sib(3)
    add(0, *R1)
    step_yh(4); step_chain(5); step_sib(4)
    q_copy(1).wait_recv()
    add(1, *R0, fresh=True)
    step_yh(5); step_chain(6); step_sib(5)
    add(1, *R1)
    step_yh(6); step_chain(7); step_sib(6)
    add(0, *R2)
    step_yh(7); step_chain(8); step_sib(7)
    add(1, *R2)
    step_yh(8); step_chain(9); step_sib(8)
    add(1, *R3)
    step_yh(9); step_sib(9)
    give(1, lambda a: acc[1, pl.ds(a * TOK, TOK), :] + part(1, a, *R4))
    q_copy(3).wait_recv()
    give(3, lambda a: part(3, a, 0, LAST + 1))
    q_copy(2).wait_recv()
    give(2, lambda a: part(2, a, 0, LAST + 1))
    add(0, 0, 15)

    for j in (1, 3, 2):
        o_copy(j).wait_recv()
        d_copy(j).wait_recv()
    for a in range(HEADS):
        rows = slice(a * TOK, (a + 1) * TOK)
        num = acc[0, rows, 0:HD]
        den = drecv[0, a:a + 1, :] + drecv[1, a:a + 1, :] + drecv[2, a:a + 1, :]
        den = jnp.sum(jnp.where(eye, den, 0.0), axis=1, keepdims=True) + acc[0, rows, HD:]
        for j in range(3):
            num = num + orecv[j, rows, :].astype(jnp.float32)
        o_ref[:, a * HD:(a + 1) * HD] = (num / den).astype(jnp.bfloat16)

    for j in (1, 2, 3):
        q_copy(j).wait_send()
        o_copy(j).wait_send()
        d_copy(j).wait_send()
    for k in range(10):
        has = L >= k if k <= 8 else (L >= k) & (c == 1)
        when(chain_send_ok(k), lambda: chain_out(k).wait_send())
        when(has & yh_ok(k, 1 - h), lambda: yh_out(k).wait_send())
        when(has & sib_ok(k, 1 - c), lambda: sib_out(k).wait_send())
        when(diag_ok(k, 1 - c), lambda: diag_out(k).wait_send())


def per_device(queries, keys, values, doc_lengths):
    vmem = pl.BlockSpec(memory_space=pltpu.VMEM)
    return pl.pallas_call(
        kernel,
        out_shape=jax.ShapeDtypeStruct((TOK, HEADS * HD), jnp.bfloat16),
        in_specs=[vmem, vmem, vmem, pl.BlockSpec(memory_space=pltpu.SMEM)],
        out_specs=vmem,
        scratch_shapes=[
            pltpu.VMEM((SLOTS * TOK, 2 * HD), jnp.bfloat16),
            pltpu.VMEM((4, ROWS, HD), jnp.bfloat16),
            pltpu.VMEM((4, TOK, TOK), jnp.int32),
            pltpu.VMEM((2, ROWS, 2 * HD), jnp.float32),
            pltpu.VMEM((3, ROWS, HD), jnp.bfloat16),
            pltpu.VMEM((3, ROWS, HD), jnp.bfloat16),
            pltpu.VMEM((3, HEADS, TOK), jnp.float32),
            pltpu.VMEM((3, HEADS, TOK), jnp.float32),
            pltpu.SemaphoreType.DMA((SLOTS,)),
            pltpu.SemaphoreType.DMA((4, 10)),
            pltpu.SemaphoreType.DMA((3,)),
            pltpu.SemaphoreType.DMA((3,)),
            pltpu.SemaphoreType.DMA((3,)),
            pltpu.SemaphoreType.DMA((3,)),
            pltpu.SemaphoreType.DMA((3,)),
            pltpu.SemaphoreType.DMA((3,)),
        ],
        compiler_params=pltpu.CompilerParams(
            collective_id=0, has_side_effects=True, vmem_limit_bytes=48 * 1024 * 1024),
        name="packed_attention",
    )(queries, keys, values, doc_lengths)


def solution(mesh):
    return jax.shard_map(
        per_device,
        mesh=mesh,
        in_specs=(
            P(("ctx", "head"), None),
            P(("ctx", "head"), None),
            P(("ctx", "head"), None),
            P(),
        ),
        out_specs=P(("ctx", "head"), None),
        check_vma=False,
    )
```

time: 329 us -> 82.8 us (0.25)
  the two profiles are of different devices: /device:TPU:168 before, /device:TPU:8 now
where the time goes in v1:
time: 82.8 us; the launch traced here: 82.5 us
  Pallas kernels  78.7 us (95%)
  local copies, waits for them, and re-layouts  3.82 us (5%)
    pallas_call x1, Pallas kernels, per_device(): pl.pallas_call(kernel, out_shape=jax.ShapeDtypeStruct((TOK, HEADS * HD),...  78.7 us
    unnamed x9, local copies, waits for them, and re-layouts  3.82 us

profile of v1, /device:TPU:8, one launch (start us, length us, event | category | flops | bytes accessed | tf_op | source)
XLA Modules:
  0.0 82.5 jit_solution(2331269316587693985)
XLA Ops:
  0.0 0.0 copy-start
  0.0 0.9 %copy-done = bf16[128,1024]{1,0:T(8,128)(2,1)S(1)} copy-done((bf16[128,1024]{1,0:T(8,128)(2,1)S(1)}, bf16[128,1024]{1,0:T(8,128)(2,1)}, u32[]{:S(2)}) %copy-start) | copy-done | bytes 262168
  1.0 0.0 copy-start.1
  1.0 0.8 copy-done.1
  1.7 0.0 copy-start.2
  1.7 0.8 copy-done.2
  2.5 0.0 copy-start.3
  2.5 0.7 copy-done.3
  3.1 78.7 %packed_attention.1 = bf16[128,1024]{1,0:T(8,128)(2,1)S(1)} custom-call(bf16[128,1024]{1,0:T(8,128)(2,1)S(1)} %copy-done, bf16[128,128]{1,0:T(8,128)(2,1)S(1)} %copy-done.1, bf16[128,128]{1,0:T(8,128)(2,1)S(1)} %copy-done.2, s32[16]{0:T(128)S(1)} %copy-done.3), custom_call_target="tpu_custom_call" | custom-call | tf_op jit(solution)/shard_map/packed_attention/pallas_call | solution.py:270
  81.8 0.7 copy.6
Async XLA Ops:
  0.0 0.9 %copy-start = (bf16[128,1024]{1,0:T(8,128)(2,1)S(1)}, bf16[128,1024]{1,0:T(8,128)(2,1)}, u32[]{:S(2)}) copy-start(bf16[128,1024]{1,0:T(8,128)(2,1)} %q_ref.1) | copy-start | bytes 786436
  1.0 0.8 copy-start.1
  1.7 0.8 copy-start.2
  2.5 0.7 copy-start.3

commit v2 on v1

--- a/solution.py
+++ b/solution.py
@@ -30,55 +30,69 @@
 
 def kernel(
     q_ref, k_ref, v_ref, len_ref, o_ref,
-    kv, qbuf, starts, acc, osend, orecv, dsend, drecv,
+    lens, local, kv, qbuf, starts, acc, osend, orecv, dsend, drecv,
     kv_recv, kv_send, q_recv, q_send, o_recv, o_send, d_recv, d_send,
 ):
     ctx = lax.axis_index("ctx")
     head = lax.axis_index("head")
     L = ctx // 2
+    z = L % 8
     c = ctx % 2
     h = head // 4
     x = head % 4
     w = 2 * c + h
     u = 4 * L + w
 
-    chain_next = (ctx + 2, head)
-    chain_prev = (ctx - 2, head)
     yh_peer = (ctx, (1 - h) * 4 + x)
     sib_peer = (L * 2 + 1 - c, head)
 
     def x_peer(j):
         return (ctx, h * 4 + (x + j) % 4)
 
-    kv[...] = jnp.zeros_like(kv)
-    kv[rows_of(LAST), 0:HD] = k_ref[...]
-    kv[rows_of(LAST), HD:] = v_ref[...]
-    for a in range(HEADS):
-        qbuf[0, a * TOK:(a + 1) * TOK, :] = q_ref[:, a * HD:(a + 1) * HD]
+    loads = [
+        pltpu.make_async_copy(k_ref, kv.at[rows_of(LAST), pl.ds(0, HD)], local.at[0]),
+        pltpu.make_async_copy(v_ref, kv.at[rows_of(LAST), pl.ds(HD, HD)], local.at[1]),
+        pltpu.make_async_copy(len_ref, lens, local.at[2]),
+    ] + [
+        pltpu.make_async_copy(
+            q_ref.at[:, pl.ds(a * HD, HD)], qbuf.at[0, pl.ds(a * TOK, TOK)], local.at[3 + a])
+        for a in range(HEADS)
+    ]
+    for load in loads:
+        load.start()
+    kv[0:(PAD + LAST) * TOK, :] = jnp.zeros(((PAD + LAST) * TOK, 2 * HD), kv.dtype)
+    kv[(PAD + LAST + 1) * TOK:, :] = jnp.zeros((TOK, 2 * HD), kv.dtype)
 
     barrier = pltpu.get_barrier_semaphore()
     for peer in (yh_peer, sib_peer, x_peer(1), x_peer(2), x_peer(3)):
         pl.semaphore_signal(barrier, inc=1, device_id=peer, device_id_type=MESH)
 
-    @pl.when(L < 15)
-    def _():
-        pl.semaphore_signal(barrier, inc=1, device_id=chain_next, device_id_type=MESH)
-
-    @pl.when(L > 0)
-    def _():
-        pl.semaphore_signal(barrier, inc=1, device_id=chain_prev, device_id_type=MESH)
+    links = [(L < 15, 1), (L > 0, -1), (L < 8, 8), (L > 7, -8)]
+    for k in (5, 6, 7):
+        links += [(z + k < 8, k), (z >= k, -k)]
+    count = jnp.int32(5)
+    for ok, away in links:
+        count = count + ok.astype(jnp.int32)
+
+        @pl.when(ok)
+        def _():
+            pl.semaphore_signal(
+                barrier, inc=1, device_id=(ctx + 2 * away, head), device_id_type=MESH)
+
+    for load in loads:
+        load.wait()
 
     for j in range(4):
         pos = (4 * u + (x + j) % 4) * TOK + lax.broadcasted_iota(jnp.int32, (TOK, TOK), 0)
         end = jnp.int32(0)
         start = jnp.zeros((TOK, TOK), jnp.int32)
         for d in range(NDOCS):
-            length = len_ref[d]
+            length = lens[d]
             end = end + length
             start = start + jnp.where(pos >= end, length, 0)
         starts[j] = start
 
-    pl.semaphore_wait(barrier, 5 + (L < 15).astype(jnp.int32) + (L > 0).astype(jnp.int32))
+    pl.semaphore_wait(barrier, count)
 
     def q_copy(j):
         return pltpu.make_async_remote_copy(
@@ -100,17 +114,25 @@
             src_ref=kv.at[rows_of(src)], dst_ref=kv.at[rows_of(dst)], send_sem=kv_send.at[kind, k],
             recv_sem=kv_recv.at[dst + PAD], device_id=peer, device_id_type=MESH)
 
-    def chain_ok(k):
-        if k == 0 or k > 9:
-            return None
-        ok = L >= k
-        return ok if k <= 8 else ok & (c == 1)
-
-    def chain_send_ok(k):
-        ok = (L >= k) & (L < 15)
-        if k + 1 <= 8:
-            return ok
-        return ok & (c == 1) if k + 1 == 9 else None
+    def owned(k):
+        return L >= k if k <= 8 else (L >= k) & (c == 1)
+
+    def out(k, to_k, away, kind, at):
+        return kv_copy(LAST - 4 * k, LAST - 4 * to_k, kind, at, (ctx + 2 * away, head))
+
+    def chain_sends(k):
+        sends = []
+        if k <= 3:
+            sends.append(((L >= k) & (L < 15), out(k, k + 1, 1, 0, k)))
+        if k == 0:
+            sends.append((L < 8, out(0, 8, 8, 0, 8)))
+            for far in (5, 6, 7):
+                sends.append((z + far < 8, out(0, far, far, 0, far)))
+        if 6 <= k <= 8:
+            sends.append(((L >= 9) & (L - k < 8) & (L >= k), out(k, k - 1, -1, 0, 9 if k == 6 else k + 3)))
+        if k == 8:
+            sends.append(((L >= 8) & (L < 15) & (c == 1), out(8, 9, 1, 0, 4)))
+        return sends
 
     def yh_ok(k, to_h):
         ok = L >= k
@@ -138,9 +160,6 @@
             return ok & (to_c == 0) & (h == 0)
         return ok
 
-    def chain_out(k):
-        return kv_copy(LAST - 4 * k, LAST - 4 * (k + 1), 0, k, chain_next)
-
     def yh_out(k):
         return kv_copy(LAST - 4 * k, LAST - 4 * k + 2 * h - 1, 1, k, yh_peer)
 
@@ -158,11 +177,12 @@
             pl.when(cond)(body)
 
     def step_chain(k):
-        when(chain_ok(k), lambda: arrived(LAST - 4 * k))
-        when(chain_send_ok(k), lambda: chain_out(k).start())
-        has = L >= k if k <= 8 else (L >= k) & (c == 1)
-        when(has & yh_ok(k, 1 - h), lambda: yh_out(k).start())
-        when(has & sib_ok(k, 1 - c), lambda: sib_out(k).start())
+        if k:
+            when(owned(k), lambda: arrived(LAST - 4 * k))
+        for ok, copy in chain_sends(k):
+            when(ok, copy.start)
+        when(owned(k) & yh_ok(k, 1 - h), lambda: yh_out(k).start())
+        when(owned(k) & sib_ok(k, 1 - c), lambda: sib_out(k).start())
 
     def step_yh(k):
         when(yh_ok(k, h), lambda: arrived(LAST - 4 * k + 1 - 2 * h))
@@ -200,7 +220,7 @@
             new = part(j, a, first, count)
             acc[j, rows, :] = new if fresh else acc[j, rows, :] + new
             return carry
-        lax.fori_loop(0, HEADS, one, 0)
+        lax.fori_loop(0, HEADS, one, 0, unroll=True)
 
     def give(j, total_of):
         def one(a, carry):
@@ -208,38 +228,55 @@
             osend[j - 1, pl.ds(a * TOK, TOK), :] = total[:, 0:HD].astype(jnp.bfloat16)
             dsend[j - 1, pl.ds(a, 1), :] = jnp.sum(jnp.where(eye, total[:, HD:], 0.0), axis=0, keepdims=True)
             return carry
-        lax.fori_loop(0, HEADS, one, 0)
+        lax.fori_loop(0, HEADS, one, 0, unroll=True)
         o_copy(j).start()
         d_copy(j).start()
-
-    R0, R1, R2, R3, R4 = (31, 4), (23, 8), (15, 8), (7, 8), (0, 7)
 
     step_chain(0)
     q_copy(1).start()
     q_copy(3).start()
-    step_yh(0); step_chain(1); step_sib(0); step_yh(1); step_chain(2); step_sib(1)
-    add(0, *R0, fresh=True)
+    step_chain(8)
+    step_chain(1)
+    step_yh(0)
+    step_chain(7)
+    step_chain(9)
+    step_chain(2)
+    step_yh(8)
+    step_yh(1)
+    step_sib(0)
+    step_sib(1)
+    add(0, 30, 5, fresh=True)
     q_copy(2).start()
-    step_yh(2); step_chain(3); step_sib(2); step_yh(3); step_chain(4); step_sib(3)
-    add(0, *R1)
-    step_yh(4); step_chain(5); step_sib(4)
+    step_chain(6)
+    step_chain(3)
+    step_yh(9)
+    step_yh(7)
+    step_yh(2)
+    for k in (8, 9, 7, 2):
+        step_sib(k)
+    add(0, 26, 4)
+    step_chain(5)
+    step_chain(4)
+    step_yh(6)
+    step_yh(3)
+    add(0, 0, 7)
+    step_yh(5)
+    step_yh(4)
     q_copy(1).wait_recv()
-    add(1, *R0, fresh=True)
-    step_yh(5); step_chain(6); step_sib(5)
-    add(1, *R1)
-    step_yh(6); step_chain(7); step_sib(6)
-    add(0, *R2)
-    step_yh(7); step_chain(8); step_sib(7)
-    add(1, *R2)
-    step_yh(8); step_chain(9); step_sib(8)
-    add(1, *R3)
-    step_yh(9); step_sib(9)
-    give(1, lambda a: acc[1, pl.ds(a * TOK, TOK), :] + part(1, a, *R4))
-    q_copy(3).wait_recv()
-    give(3, lambda a: part(3, a, 0, LAST + 1))
-    q_copy(2).wait_recv()
-    give(2, lambda a: part(2, a, 0, LAST + 1))
-    add(0, 0, 15)
+    add(1, 26, 9, fresh=True)
+    add(1, 0, 7)
+    for k in (6, 3, 5, 4):
+        step_sib(k)
+    give(1, lambda a: acc[1, pl.ds(a * TOK, TOK), :] + part(1, a, 7, 19))
+
+    def whole(i, carry):
+        j = 3 - i
+        q_copy(j).wait_recv()
+        give(j, lambda a: part(j, a, 0, LAST + 1))
+        return carry
+
+    lax.fori_loop(0, 2, whole, 0)
+    add(0, 7, 19)
 
     for j in (1, 3, 2):
         o_copy(j).wait_recv()
@@ -258,21 +295,22 @@
         o_copy(j).wait_send()
         d_copy(j).wait_send()
     for k in range(10):
-        has = L >= k if k <= 8 else (L >= k) & (c == 1)
-        when(chain_send_ok(k), lambda: chain_out(k).wait_send())
-        when(has & yh_ok(k, 1 - h), lambda: yh_out(k).wait_send())
-        when(has & sib_ok(k, 1 - c), lambda: sib_out(k).wait_send())
+        for ok, copy in chain_sends(k):
+            when(ok, copy.wait_send)
+        when(owned(k) & yh_ok(k, 1 - h), lambda: yh_out(k).wait_send())
+        when(owned(k) & sib_ok(k, 1 - c), lambda: sib_out(k).wait_send())
         when(diag_ok(k, 1 - c), lambda: diag_out(k).wait_send())
 
 
 def per_device(queries, keys, values, doc_lengths):
-    vmem = pl.BlockSpec(memory_space=pltpu.VMEM)
     return pl.pallas_call(
         kernel,
         out_shape=jax.ShapeDtypeStruct((TOK, HEADS * HD), jnp.bfloat16),
-        in_specs=[vmem, vmem, vmem, pl.BlockSpec(memory_space=pltpu.SMEM)],
-        out_specs=vmem,
+        in_specs=[pl.BlockSpec(memory_space=pl.ANY)] * 4,
+        out_specs=pl.BlockSpec(memory_space=pltpu.VMEM),
         scratch_shapes=[
+            pltpu.SMEM((NDOCS,), jnp.int32),
+            pltpu.SemaphoreType.DMA((3 + HEADS,)),
             pltpu.VMEM((SLOTS * TOK, 2 * HD), jnp.bfloat16),
             pltpu.VMEM((4, ROWS, HD), jnp.bfloat16),
             pltpu.VMEM((4, TOK, TOK), jnp.int32),
@@ -282,7 +320,7 @@
             pltpu.VMEM((3, HEADS, TOK), jnp.float32),
             pltpu.VMEM((3, HEADS, TOK), jnp.float32),
             pltpu.SemaphoreType.DMA((SLOTS,)),
-            pltpu.SemaphoreType.DMA((4, 10)),
+            pltpu.SemaphoreType.DMA((4, 12)),
             pltpu.SemaphoreType.DMA((3,)),
             pltpu.SemaphoreType.DMA((3,)),
             pltpu.SemaphoreType.DMA((3,)),
@@ -291,7 +329,7 @@
             pltpu.SemaphoreType.DMA((3,)),
         ],
         compiler_params=pltpu.CompilerParams(
-            collective_id=0, has_side_effects=True, vmem_limit_bytes=48 * 1024 * 1024),
+            collective_id=0, has_side_effects=True, vmem_limit_bytes=60 * 1024 * 1024),
         name="packed_attention",
     )(queries, keys, values, doc_lengths)
 

time: 82.8 us -> 59 us (0.71)
  Pallas kernels: 78.7 us -> 57.1 us
  local copies, waits for them, and re-layouts: 3.82 us -> 1.67 us
    pallas_call x1, Pallas kernels: 78.7 us -> 57.1 us  [per_device(): pl.pallas_call(kernel, out_shape=jax.ShapeDtypeStruct((TOK, HEADS * HD),...]
    unnamed x9 -> x1, local copies, waits for them, and re-layouts: 3.82 us -> 1.67 us
where the time goes in v2:
time: 59 us; the launch traced here: 58.8 us
  Pallas kernels  57.1 us (97%)
  local copies, waits for them, and re-layouts  1.67 us (3%)
    pallas_call x1, Pallas kernels, per_device(): pl.pallas_call(kernel, out_shape=jax.ShapeDtypeStruct((TOK, HEADS * HD),...  57.1 us
    unnamed x1, local copies, waits for them, and re-layouts  1.67 us

profile of v2, /device:TPU:8, one launch (start us, length us, event | category | flops | bytes accessed | tf_op | source)
XLA Modules:
  0.0 58.8 jit_solution(9308110807843464443)
XLA Ops:
  0.0 57.1 %packed_attention.1 = bf16[128,1024]{1,0:T(8,128)(2,1)} custom-call(bf16[128,1024]{1,0:T(8,128)(2,1)} %q_ref.1, bf16[128,128]{1,0:T(8,128)(2,1)} %k_ref.1, bf16[128,128]{1,0:T(8,128)(2,1)} %v_ref.1, s32[16]{0:T(128)} %len_ref.1), custom_call_target="tpu_custom_call" | custom-call | tf_op jit(solution)/shard_map/packed_attention/pallas_call | solution.py:306
  57.2 1.7 %copy.6 = bf16[128,1024]{1,0:T(8,128)(2,1)} copy(bf16[128,1024]{1,0:T(8,128)(2,1)} %packed_attention.1) | data formatting | bytes 524288

commit v3 on v2

v3 whole, which is shorter than its diff:
```python
import functools
import math

import jax
import jax.numpy as jnp
from jax import lax
from jax.experimental import pallas as pl
from jax.experimental.pallas import tpu as pltpu
from jax.sharding import PartitionSpec as P

MESH = pl.DeviceIdType.MESH
HD = 128
HEADS = 8
TOK = 128
NDOCS = 16
ROWS = HEADS * TOK
FACTOR = 1.0 / (30.0 * math.sqrt(HD))
GAIN = 30.0 * math.log2(math.e)
OWN, SIB, YH, DIAG = range(4)
ACROSS = (1, 8)
ORDER = (0, 1, 8, 2, 7, 3, 6, 4, 5)
EARLY = [(g, p) for g in (OWN, SIB) for p in (0, 1, 2)] + [(g, p) for g in (OWN, SIB) for p in (3, 4)]
EARLY += [(g, p) for g in (YH, DIAG) for p in (0, 1, 2)] + [(g, p) for g in (YH, DIAG) for p in (3, 4)]
LATE = [(g, p) for g in (OWN, SIB, YH, DIAG) for p in (5, 6)]
LATE += [(g, p) for g in (OWN, SIB, YH, DIAG) for p in (7, 8)]
SLOT = EARLY + LATE + [(OWN, 9), (YH, 9)]


def place(g, k):
    if k == 9:
        return SLOT.index((g, 9 if g in (OWN, YH) else 0))
    return SLOT.index((g, ORDER.index(k)))


def rows_of(slot, count=1):
    return pl.ds(slot * TOK, count * TOK)


def kernel(
    q_ref, k_ref, v_ref, len_ref, o_ref,
    lens, local, kv, qbuf, starts, acc, osend, orecv, dsend, drecv,
    kv_recv, kv_send, q_recv, q_send, o_recv, o_send, d_recv, d_send,
):
    ctx = lax.axis_index("ctx")
    head = lax.axis_index("head")
    L = ctx // 2
    z = L % 8
    c = ctx % 2
    h = head // 4
    x = head % 4
    w = 2 * c + h
    u = 4 * L + w

    other = (1 - h) * 4 + x
    yh_peer = (ctx, other)
    sib_peer = (L * 2 + 1 - c, head)

    def x_peer(j):
        return (ctx, h * 4 + (x + j) % 4)

    barrier = pltpu.get_barrier_semaphore()
    for peer in (yh_peer, sib_peer, x_peer(1), x_peer(2), x_peer(3)):
        pl.semaphore_signal(barrier, inc=1, device_id=peer, device_id_type=MESH)

    count = jnp.int32(5)
    for away in range(1, 10):
        from_ok, to_ok = L >= away, L + away < 16
        if away == 9:
            from_ok, to_ok = from_ok & (c == 1), to_ok & (c == 1)
        peers = [head] * (away not in (3, 4)) + [other] * (away in ACROSS)
        count = count + len(peers) * to_ok.astype(jnp.int32)

        @pl.when(from_ok)
        def _():
            for peer in peers:
                pl.semaphore_signal(
                    barrier, inc=1, device_id=(ctx - 2 * away, peer), device_id_type=MESH)

    loads = [
        pltpu.make_async_copy(k_ref, kv.at[rows_of(0), pl.ds(0, HD)], local.at[0]),
        pltpu.make_async_copy(v_ref, kv.at[rows_of(0), pl.ds(HD, HD)], local.at[1]),
        pltpu.make_async_copy(len_ref, lens, local.at[2]),
    ] + [
        pltpu.make_async_copy(
            q_ref.at[:, pl.ds(a * HD, HD)], qbuf.at[0, pl.ds(a * TOK, TOK)], local.at[3 + a])
        for a in range(HEADS)
    ]
    for load in loads:
        load.start()

    for slot, (g, p) in enumerate(EARLY + LATE):
        empty = L < ORDER[p]
        if p == 0 and g == SIB:
            empty = (c == 0) & (L < 9)
        if p == 0 and g == DIAG:
            empty = (c == 0) & ((L < 9) | (h == 1))
        if p == 0 and g in (OWN, YH):
            continue

        @pl.when(empty)
        def _():
            kv[rows_of(slot), :] = jnp.zeros((TOK, 2 * HD), kv.dtype)

    for load in loads:
        load.wait()

    pl.semaphore_wait(barrier, count)

    def q_copy(j):
        return pltpu.make_async_remote_copy(
            src_ref=qbuf.at[0], dst_ref=qbuf.at[j], send_sem=q_send.at[j - 1],
            recv_sem=q_recv.at[j - 1], device_id=x_peer(4 - j), device_id_type=MESH)

    def o_copy(j, half):
        rows = pl.ds(half * (ROWS // 2), ROWS // 2)
        return pltpu.make_async_remote_copy(
            src_ref=osend.at[j - 1, rows], dst_ref=orecv.at[j - 1, rows], send_sem=o_send.at[j - 1, half],
            recv_sem=o_recv.at[j - 1, half], device_id=x_peer(j if j != 2 else 1 + 2 * half),
            device_id_type=MESH)

    def d_copy(j):
        return pltpu.make_async_remote_copy(
            src_ref=dsend.at[j - 1], dst_ref=drecv.at[j - 1], send_sem=d_send.at[j - 1],
            recv_sem=d_recv.at[j - 1], device_id=x_peer(j), device_id_type=MESH)

    def kv_copy(src, dst, kind, k, peer):
        return pltpu.make_async_remote_copy(
            src_ref=kv.at[rows_of(src)], dst_ref=kv.at[rows_of(dst)], send_sem=kv_send.at[kind, k],
            recv_sem=kv_recv.at[dst], device_id=peer, device_id_type=MESH)

    def owned(k):
        return L >= k if k <= 8 else (L >= k) & (c == 1)

    def out(k, to_k, across=False):
        return kv_copy(
            place(OWN, k), place(YH if across else OWN, to_k), 1 if across else 0, to_k,
            (ctx + 2 * (to_k - k), other if across else head))

    def first_sends():
        sends = [(L + 1 < 16, out(0, 1)), (L + 8 < 16, out(0, 8))]
        sends += [(L + 1 < 16, out(0, 1, True)), (L + 8 < 16, out(0, 8, True))]
        sends += [(L + 2 < 16, out(0, 2)), (L + 7 < 16, out(0, 7)), ((L + 9 < 16) & (c == 1), out(0, 9))]
        return sends

    def second_sends():
        return [(L + 6 < 16, out(0, 6)), (L + 5 < 16, out(0, 5))]

    def third_sends():
        return [((L >= 2) & (L + 1 < 16), out(2, 3)), ((L >= 2) & (L + 2 < 16), out(2, 4))]

    def yh_ok(k, to_h):
        return L >= k if k <= 8 else (L >= k) & (c == 1) & (to_h == 0)

    def sib_ok(k, to_c):
        if k in (0, 9):
            return (L >= k) & (to_c == (0 if k else 1))
        return L >= k

    def diag_ok(k, to_c):
        if k == 0:
            return to_c == 1
        return L >= k if k <= 8 else (L >= k) & (to_c == 0) & (h == 0)

    def yh_out(k):
        return kv_copy(place(OWN, k), place(YH, k), 1, k, yh_peer)

    def sib_out(k):
        return kv_copy(place(OWN, k), place(SIB, k), 2, k, sib_peer)

    def diag_out(k):
        return kv_copy(place(YH, k), place(DIAG, k), 3, k, sib_peer)

    def arrived(slot):
        kv_copy(slot, slot, 0, 0, sib_peer).wait_recv()

    def send(sends):
        for ok, copy in sends:
            pl.when(ok)(copy.start)

    def step_own(k):
        if k:
            pl.when(owned(k))(lambda: arrived(place(OWN, k)))
        if k == 2:
            send(third_sends())
        if k not in ACROSS:
            pl.when(owned(k) & yh_ok(k, 1 - h))(lambda: yh_out(k).start())
        pl.when(owned(k) & sib_ok(k, 1 - c))(lambda: sib_out(k).start())

    def step_yh(k):
        pl.when(yh_ok(k, h))(lambda: arrived(place(YH, k)))
        pl.when(diag_ok(k, 1 - c))(lambda: diag_out(k).start())

    def step_sib(*ks):
        for k in ks:
            pl.when(sib_ok(k, c))(lambda: arrived(place(SIB, k)))

    def step_diag(*ks):
        for k in ks:
            pl.when(diag_ok(k, c))(lambda: arrived(place(DIAG, k)))

    lane = lax.broadcasted_iota(jnp.int32, (TOK, TOK), 1)
    sub = lax.broadcasted_iota(jnp.int32, (TOK, TOK), 0)
    eye = lane == sub

    def part(j, a, first, count):
        q = qbuf[j, pl.ds(a * TOK, TOK), :]
        k = kv[rows_of(first, count), 0:HD]
        v = kv[rows_of(first, count), HD:]
        v = jnp.concatenate([v, jnp.ones_like(v)], axis=1)
        s = lax.dot_general(q, k, (((1,), (1,)), ((), ())), preferred_element_type=jnp.float32)
        p = jnp.exp2(jnp.tanh(s * FACTOR) * GAIN)
        start = starts[j]
        tiles = []
        for t in range(count):
            g, at = SLOT[first + t]
            k_of = 9 * (1 - c) if at == 0 and g in (SIB, DIAG) else ORDER[at]
            w_of = w + (1 - 2 * h if g in (YH, DIAG) else 0) + (2 - 4 * c if g in (SIB, DIAG) else 0)
            key_pos = (4 * (4 * (L - k_of) + w_of) + x) * TOK + lane
            ok = key_pos >= start
            if at == 0:
                ok = ok & (key_pos <= (4 * u + (x + j) % 4) * TOK + sub)
            tiles.append(jnp.where(ok, p[:, t * TOK:(t + 1) * TOK], 0.0).astype(jnp.bfloat16))
        return jnp.dot(jnp.concatenate(tiles, axis=1), v, preferred_element_type=jnp.float32)

    def add(j, first, count, fresh=False, heads=(0, HEADS)):
        def one(a, carry):
            rows = pl.ds(a * TOK, TOK)
            new = part(j, a, first, count)
            acc[j, rows, :] = new if fresh else acc[j, rows, :] + new
            return carry
        lax.fori_loop(*heads, one, 0, unroll=True)

    def give(j, half, first=None, count=0, passing=False):
        def one(a, carry):
            rows = pl.ds(a * TOK, TOK)
            total = acc[j, rows, :]
            if count:
                total = total + part(j, a, first, count)
            numerator = total[:, 0:HD]
            if passing:
                numerator = numerator + orecv[1, rows, :].astype(jnp.float32)
            osend[j - 1, rows, :] = numerator.astype(jnp.bfloat16)
            dsend[j - 1, pl.ds(a, 1), :] = jnp.sum(jnp.where(eye, total[:, HD:], 0.0), axis=0, keepdims=True)
            return carry
        lax.fori_loop(half * HEADS // 2, (half + 1) * HEADS // 2, one, 0, unroll=True)
        o_copy(j, half).start()

    def others(first, count, hooks, fresh=False):
        def one(i, carry):
            j = 1 + (2 * i) % 3
            if fresh:
                q_copy(j).wait_recv()
            add(j, first, count, fresh)
            for at, hook in enumerate(hooks):
                pl.when(i == at)(hook)
            return carry
        lax.fori_loop(0, 3, one, 0)

    def steps(*pairs):
        def run():
            for step, k in pairs:
                step(k)
        return run

    send(first_sends())
    step_own(0)
    q_copy(1).start()
    q_copy(3).start()

    for j in range(4):
        pos = (4 * u + (x + j) % 4) * TOK + lax.broadcasted_iota(jnp.int32, (TOK, TOK), 0)
        end = jnp.int32(0)
        start = jnp.zeros((TOK, TOK), jnp.int32)
        for d in range(NDOCS):
            length = lens[d]
            end = end + length
            start = start + jnp.where(pos >= end, length, 0)
        starts[j] = start

    step_own(1)
    step_own(8)
    step_sib(0, 1, 8)
    step_own(9)
    step_sib(9)
    add(0, 0, 6, fresh=True)
    q_copy(2).start()
    step_yh(0)
    step_yh(1)
    step_yh(8)
    step_own(2)
    step_own(7)
    send(second_sends())
    step_sib(2, 7)
    add(0, 6, 4)
    others(0, 10, [
        steps((step_yh, 9), (step_yh, 2), (step_yh, 7)),
        steps((step_own, 3), (step_own, 6)),
        steps((step_diag, 0), (step_diag, 1), (step_diag, 8), (step_diag, 9), (step_diag, 2), (step_diag, 7)),
    ], fresh=True)
    others(10, 10, [
        steps((step_own, 5), (step_own, 4)),
        steps((step_yh, 3), (step_yh, 6)),
        steps((step_sib, 3), (step_sib, 6), (step_diag, 3), (step_diag, 6)),
    ])
    others(20, 8, [
        steps((step_yh, 5), (step_yh, 4)),
        steps(),
        steps((step_sib, 4), (step_sib, 5), (step_diag, 4), (step_diag, 5)),
    ])

    give(2, 0, 28, 8)
    give(2, 1, 28, 8)
    d_copy(2).start()
    give(1, 1, 28, 8)
    give(3, 0, 28, 8)
    add(1, 28, 8, heads=(0, HEADS // 2))
    add(3, 28, 8, heads=(HEADS // 2, HEADS))
    add(0, 10, 10)
    o_copy(2, 0).wait_recv()
    give(1, 0, passing=True)
    o_copy(2, 1).wait_recv()
    give(3, 1, passing=True)
    d_copy(1).start()
    d_copy(3).start()
    add(0, 20, 16)

    for j in (2, 3, 1):
        d_copy(j).wait_recv()
    for a in range(HEADS):
        if a % (HEADS // 2) == 0:
            for j in (1, 3):
                o_copy(j, a // (HEADS // 2)).wait_recv()
        rows = slice(a * TOK, (a + 1) * TOK)
        num = acc[0, rows, 0:HD]
        den = drecv[0, a:a + 1, :] + drecv[1, a:a + 1, :] + drecv[2, a:a + 1, :]
        den = jnp.sum(jnp.where(eye, den, 0.0), axis=1, keepdims=True) + acc[0, rows, HD:]
        for j in (0, 2):
            num = num + orecv[j, rows, :].astype(jnp.float32)
        o_ref[:, a * HD:(a + 1) * HD] = (num / den).astype(jnp.bfloat16)

    for j in (1, 2, 3):
        q_copy(j).wait_send()
        o_copy(j, 0).wait_send()
        o_copy(j, 1).wait_send()
        d_copy(j).wait_send()
    for ok, copy in first_sends() + second_sends() + third_sends():
        pl.when(ok)(copy.wait_send)
    for k in range(10):
        if k not in ACROSS:
            pl.when(owned(k) & yh_ok(k, 1 - h))(lambda: yh_out(k).wait_send())
        pl.when(owned(k) & sib_ok(k, 1 - c))(lambda: sib_out(k).wait_send())
        pl.when(diag_ok(k, 1 - c))(lambda: diag_out(k).wait_send())


def per_device(queries, keys, values, doc_lengths):
    return pl.pallas_call(
        kernel,
        out_shape=jax.ShapeDtypeStruct((TOK, HEADS * HD), jnp.bfloat16),
        in_specs=[pl.BlockSpec(memory_space=pl.ANY)] * 4,
        out_specs=pl.BlockSpec(memory_space=pltpu.VMEM),
        scratch_shapes=[
            pltpu.SMEM((NDOCS,), jnp.int32),
            pltpu.SemaphoreType.DMA((3 + HEADS,)),
            pltpu.VMEM((len(SLOT) * TOK, 2 * HD), jnp.bfloat16),
            pltpu.VMEM((4, ROWS, HD), jnp.bfloat16),
            pltpu.VMEM((4, TOK, TOK), jnp.int32),
            pltpu.VMEM((4, ROWS, 2 * HD), jnp.float32),
            pltpu.VMEM((3, ROWS, HD), jnp.bfloat16),
            pltpu.VMEM((3, ROWS, HD), jnp.bfloat16),
            pltpu.VMEM((3, HEADS, TOK), jnp.float32),
            pltpu.VMEM((3, HEADS, TOK), jnp.float32),
            pltpu.SemaphoreType.DMA((len(SLOT),)),
            pltpu.SemaphoreType.DMA((4, 10)),
            pltpu.SemaphoreType.DMA((3,)),
            pltpu.SemaphoreType.DMA((3,)),
            pltpu.SemaphoreType.DMA((3, 2)),
            pltpu.SemaphoreType.DMA((3, 2)),
            pltpu.SemaphoreType.DMA((3,)),
            pltpu.SemaphoreType.DMA((3,)),
        ],
        compiler_params=pltpu.CompilerParams(
            collective_id=0, has_side_effects=True, vmem_limit_bytes=40 * 1024 * 1024),
        name="packed_attention",
    )(queries, keys, values, doc_lengths)


def solution(mesh):
    return jax.shard_map(
        per_device,
        mesh=mesh,
        in_specs=(
            P(("ctx", "head"), None),
            P(("ctx", "head"), None),
            P(("ctx", "head"), None),
            P(),
        ),
        out_specs=P(("ctx", "head"), None),
        check_vma=False,
    )
```

time: 59 us -> 54.1 us (0.917)
  Pallas kernels: 57.1 us -> 50 us
  local copies, waits for them, and re-layouts: 1.67 us -> 3.82 us
    pallas_call x1, Pallas kernels: 57.1 us -> 50 us  [per_device(): pl.pallas_call(kernel, out_shape=jax.ShapeDtypeStruct((TOK, HEADS * HD),...]
    unnamed x1 -> x9, local copies, waits for them, and re-layouts: 1.67 us -> 3.82 us
where the time goes in v3:
time: 54.1 us; the launch traced here: 53.9 us
  Pallas kernels  50 us (92%)
  local copies, waits for them, and re-layouts  3.82 us (7%)
    pallas_call x1, Pallas kernels, per_device(): pl.pallas_call(kernel, out_shape=jax.ShapeDtypeStruct((TOK, HEADS * HD),...  50 us
    unnamed x9, local copies, waits for them, and re-layouts  3.82 us

profile of v3, /device:TPU:8, one launch (start us, length us, event | category | flops | bytes accessed | tf_op | source)
XLA Modules:
  0.0 53.9 jit_solution(6521337915120908146)
XLA Ops:
  0.0 0.0 copy-start
  0.0 0.9 %copy-done = bf16[128,1024]{1,0:T(8,128)(2,1)S(1)} copy-done((bf16[128,1024]{1,0:T(8,128)(2,1)S(1)}, bf16[128,1024]{1,0:T(8,128)(2,1)}, u32[]{:S(2)}) %copy-start) | copy-done | bytes 262168
  1.0 0.0 copy-start.1
  1.0 0.8 %copy-done.1 = bf16[128,128]{1,0:T(8,128)(2,1)S(1)} copy-done((bf16[128,128]{1,0:T(8,128)(2,1)S(1)}, bf16[128,128]{1,0:T(8,128)(2,1)}, u32[]{:S(2)}) %copy-start.1) | copy-done | bytes 32792
  1.7 0.0 copy-start.2
  1.7 0.8 %copy-done.2 = bf16[128,128]{1,0:T(8,128)(2,1)S(1)} copy-done((bf16[128,128]{1,0:T(8,128)(2,1)S(1)}, bf16[128,128]{1,0:T(8,128)(2,1)}, u32[]{:S(2)}) %copy-start.2) | copy-done | bytes 32792
  2.5 0.0 copy-start.3
  2.5 0.7 %copy-done.3 = s32[16]{0:T(128)S(1)} copy-done((s32[16]{0:T(128)S(1)}, s32[16]{0:T(128)}, u32[]{:S(2)}) %copy-start.3) | copy-done | bytes 88
  3.1 50.0 %packed_attention.1 = bf16[128,1024]{1,0:T(8,128)(2,1)S(1)} custom-call(bf16[128,1024]{1,0:T(8,128)(2,1)S(1)} %copy-done, bf16[128,128]{1,0:T(8,128)(2,1)S(1)} %copy-done.1, bf16[128,128]{1,0:T(8,128)(2,1)S(1)} %copy-done.2, s32[16]{0:T(128)S(1)} %copy-done.3), custom_call_target="tpu_custom_call" | custom-call | tf_op jit(solution)/shard_map/packed_attention/pallas_call | solution.py:356
  53.2 0.7 %copy.6 = bf16[128,1024]{1,0:T(8,128)(2,1)} copy(bf16[128,1024]{1,0:T(8,128)(2,1)S(1)} %packed_attention.1) | data formatting | bytes 524288
Async XLA Ops:
  0.0 0.9 %copy-start = (bf16[128,1024]{1,0:T(8,128)(2,1)S(1)}, bf16[128,1024]{1,0:T(8,128)(2,1)}, u32[]{:S(2)}) copy-start(bf16[128,1024]{1,0:T(8,128)(2,1)} %q_ref.1) | copy-start | bytes 786436
  1.0 0.8 %copy-start.1 = (bf16[128,128]{1,0:T(8,128)(2,1)S(1)}, bf16[128,128]{1,0:T(8,128)(2,1)}, u32[]{:S(2)}) copy-start(bf16[128,128]{1,0:T(8,128)(2,1)} %k_ref.1) | copy-start | bytes 98308
  1.7 0.8 %copy-start.2 = (bf16[128,128]{1,0:T(8,128)(2,1)S(1)}, bf16[128,128]{1,0:T(8,128)(2,1)}, u32[]{:S(2)}) copy-start(bf16[128,128]{1,0:T(8,128)(2,1)} %v_ref.1) | copy-start | bytes 98308
  2.5 0.7 %copy-start.3 = (s32[16]{0:T(128)S(1)}, s32[16]{0:T(128)}, u32[]{:S(2)}) copy-start(s32[16]{0:T(128)} %len_ref.1) | copy-start | bytes 196

commit v4 on v3

--- a/solution.py
+++ b/solution.py
@@ -247,14 +247,14 @@
 
     def others(first, count, hooks, fresh=False):
         def one(i, carry):
-            j = 1 + (2 * i) % 3
+            j = 1 + 2 * i
             if fresh:
                 q_copy(j).wait_recv()
             add(j, first, count, fresh)
             for at, hook in enumerate(hooks):
                 pl.when(i == at)(hook)
             return carry
-        lax.fori_loop(0, 3, one, 0)
+        lax.fori_loop(0, 2, one, 0)
 
     def steps(*pairs):
         def run():
@@ -295,27 +295,27 @@
     others(0, 10, [
         steps((step_yh, 9), (step_yh, 2), (step_yh, 7)),
         steps((step_own, 3), (step_own, 6)),
-        steps((step_diag, 0), (step_diag, 1), (step_diag, 8), (step_diag, 9), (step_diag, 2), (step_diag, 7)),
     ], fresh=True)
+    step_diag(0, 1, 8, 9, 2, 7)
     others(10, 10, [
         steps((step_own, 5), (step_own, 4)),
         steps((step_yh, 3), (step_yh, 6)),
-        steps((step_sib, 3), (step_sib, 6), (step_diag, 3), (step_diag, 6)),
     ])
-    others(20, 8, [
-        steps((step_yh, 5), (step_yh, 4)),
-        steps(),
-        steps((step_sib, 4), (step_sib, 5), (step_diag, 4), (step_diag, 5)),
-    ])
-
-    give(2, 0, 28, 8)
-    give(2, 1, 28, 8)
+    q_copy(2).wait_recv()
+    add(2, 0, 20, fresh=True)
+    steps((step_yh, 5), (step_yh, 4))()
+    step_sib(3, 6)
+    step_diag(3, 6)
+    add(0, 10, 10)
+    step_sib(4, 5)
+    step_diag(4, 5)
+    give(2, 0, 20, 16)
+    give(2, 1, 20, 16)
     d_copy(2).start()
-    give(1, 1, 28, 8)
-    give(3, 0, 28, 8)
-    add(1, 28, 8, heads=(0, HEADS // 2))
-    add(3, 28, 8, heads=(HEADS // 2, HEADS))
-    add(0, 10, 10)
+    give(1, 1, 20, 16)
+    give(3, 0, 20, 16)
+    add(1, 20, 16, heads=(0, HEADS // 2))
+    add(3, 20, 16, heads=(HEADS // 2, HEADS))
     o_copy(2, 0).wait_recv()
     give(1, 0, passing=True)
     o_copy(2, 1).wait_recv()

time: 54.1 us -> 54.5 us (level)
  the two profiles are of different devices: /device:TPU:8 before, /device:TPU:41 now
where the time goes in v4:
time: 54.5 us; the launch traced here: 54.3 us
  Pallas kernels  50.5 us (93%)
  local copies, waits for them, and re-layouts  3.82 us (7%)
    pallas_call x1, Pallas kernels, per_device(): pl.pallas_call(kernel, out_shape=jax.ShapeDtypeStruct((TOK, HEADS * HD),...  50.5 us
    unnamed x9, local copies, waits for them, and re-layouts  3.82 us

profile of v4, /device:TPU:41, one launch (start us, length us, event | category | flops | bytes accessed | tf_op | source)
XLA Modules:
  0.0 54.3 jit_solution(2829213732055016447)
XLA Ops:
  0.0 0.0 copy-start
  0.0 0.9 %copy-done = bf16[128,1024]{1,0:T(8,128)(2,1)S(1)} copy-done((bf16[128,1024]{1,0:T(8,128)(2,1)S(1)}, bf16[128,1024]{1,0:T(8,128)(2,1)}, u32[]{:S(2)}) %copy-start) | copy-done | bytes 262168
  1.0 0.0 copy-start.1
  1.0 0.8 %copy-done.1 = bf16[128,128]{1,0:T(8,128)(2,1)S(1)} copy-done((bf16[128,128]{1,0:T(8,128)(2,1)S(1)}, bf16[128,128]{1,0:T(8,128)(2,1)}, u32[]{:S(2)}) %copy-start.1) | copy-done | bytes 32792
  1.7 0.0 copy-start.2
  1.7 0.8 %copy-done.2 = bf16[128,128]{1,0:T(8,128)(2,1)S(1)} copy-done((bf16[128,128]{1,0:T(8,128)(2,1)S(1)}, bf16[128,128]{1,0:T(8,128)(2,1)}, u32[]{:S(2)}) %copy-start.2) | copy-done | bytes 32792
  2.5 0.0 copy-start.3
  2.5 0.7 %copy-done.3 = s32[16]{0:T(128)S(1)} copy-done((s32[16]{0:T(128)S(1)}, s32[16]{0:T(128)}, u32[]{:S(2)}) %copy-start.3) | copy-done | bytes 88
  3.1 50.5 %packed_attention.1 = bf16[128,1024]{1,0:T(8,128)(2,1)S(1)} custom-call(bf16[128,1024]{1,0:T(8,128)(2,1)S(1)} %copy-done, bf16[128,128]{1,0:T(8,128)(2,1)S(1)} %copy-done.1, bf16[128,128]{1,0:T(8,128)(2,1)S(1)} %copy-done.2, s32[16]{0:T(128)S(1)} %copy-done.3), custom_call_target="tpu_custom_call" | custom-call | tf_op jit(solution)/shard_map/packed_attention/pallas_call | solution.py:356
  53.6 0.7 %copy.6 = bf16[128,1024]{1,0:T(8,128)(2,1)} copy(bf16[128,1024]{1,0:T(8,128)(2,1)S(1)} %packed_attention.1) | data formatting | bytes 524288
Async XLA Ops:
  0.0 0.9 %copy-start = (bf16[128,1024]{1,0:T(8,128)(2,1)S(1)}, bf16[128,1024]{1,0:T(8,128)(2,1)}, u32[]{:S(2)}) copy-start(bf16[128,1024]{1,0:T(8,128)(2,1)} %q_ref.1) | copy-start | bytes 786436
  1.0 0.8 %copy-start.1 = (bf16[128,128]{1,0:T(8,128)(2,1)S(1)}, bf16[128,128]{1,0:T(8,128)(2,1)}, u32[]{:S(2)}) copy-start(bf16[128,128]{1,0:T(8,128)(2,1)} %k_ref.1) | copy-start | bytes 98308
  1.7 0.8 %copy-start.2 = (bf16[128,128]{1,0:T(8,128)(2,1)S(1)}, bf16[128,128]{1,0:T(8,128)(2,1)}, u32[]{:S(2)}) copy-start(bf16[128,128]{1,0:T(8,128)(2,1)} %v_ref.1) | copy-start | bytes 98308
  2.5 0.7 %copy-start.3 = (s32[16]{0:T(128)S(1)}, s32[16]{0:T(128)}, u32[]{:S(2)}) copy-start(s32[16]{0:T(128)} %len_ref.1) | copy-start | bytes 196

commit v5 on v3

--- a/solution.py
+++ b/solution.py
@@ -215,10 +215,10 @@
             g, at = SLOT[first + t]
             k_of = 9 * (1 - c) if at == 0 and g in (SIB, DIAG) else ORDER[at]
             w_of = w + (1 - 2 * h if g in (YH, DIAG) else 0) + (2 - 4 * c if g in (SIB, DIAG) else 0)
-            key_pos = (4 * (4 * (L - k_of) + w_of) + x) * TOK + lane
-            ok = key_pos >= start
+            key_pos = (4 * (4 * (L - k_of) + w_of) + x) * TOK
+            ok = start <= key_pos
             if at == 0:
-                ok = ok & (key_pos <= (4 * u + (x + j) % 4) * TOK + sub)
+                ok = ok & (lane - sub <= (4 * u + (x + j) % 4) * TOK - key_pos)
             tiles.append(jnp.where(ok, p[:, t * TOK:(t + 1) * TOK], 0.0).astype(jnp.bfloat16))
         return jnp.dot(jnp.concatenate(tiles, axis=1), v, preferred_element_type=jnp.float32)
 
@@ -275,7 +275,7 @@
             length = lens[d]
             end = end + length
             start = start + jnp.where(pos >= end, length, 0)
-        starts[j] = start
+        starts[j] = start - lane
 
     step_own(1)
     step_own(8)

time: 54.1 us -> 54.1 us (level)
  no operation moved by 1% of the time
where the time goes in v5:
time: 54.1 us; the launch traced here: 53.9 us
  Pallas kernels  50 us (92%)
  local copies, waits for them, and re-layouts  3.82 us (7%)
    pallas_call x1, Pallas kernels, per_device(): pl.pallas_call(kernel, out_shape=jax.ShapeDtypeStruct((TOK, HEADS * HD),...  50 us
    unnamed x9, local copies, waits for them, and re-layouts  3.82 us

profile of v5, /device:TPU:8, one launch (start us, length us, event | category | flops | bytes accessed | tf_op | source)
XLA Modules:
  0.0 53.9 jit_solution(10650390704685933055)
XLA Ops:
  0.0 0.0 copy-start
  0.0 0.9 %copy-done = bf16[128,1024]{1,0:T(8,128)(2,1)S(1)} copy-done((bf16[128,1024]{1,0:T(8,128)(2,1)S(1)}, bf16[128,1024]{1,0:T(8,128)(2,1)}, u32[]{:S(2)}) %copy-start) | copy-done | bytes 262168
  1.0 0.0 copy-start.1
  1.0 0.8 %copy-done.1 = bf16[128,128]{1,0:T(8,128)(2,1)S(1)} copy-done((bf16[128,128]{1,0:T(8,128)(2,1)S(1)}, bf16[128,128]{1,0:T(8,128)(2,1)}, u32[]{:S(2)}) %copy-start.1) | copy-done | bytes 32792
  1.7 0.0 copy-start.2
  1.7 0.8 %copy-done.2 = bf16[128,128]{1,0:T(8,128)(2,1)S(1)} copy-done((bf16[128,128]{1,0:T(8,128)(2,1)S(1)}, bf16[128,128]{1,0:T(8,128)(2,1)}, u32[]{:S(2)}) %copy-start.2) | copy-done | bytes 32792
  2.5 0.0 copy-start.3
  2.5 0.7 %copy-done.3 = s32[16]{0:T(128)S(1)} copy-done((s32[16]{0:T(128)S(1)}, s32[16]{0:T(128)}, u32[]{:S(2)}) %copy-start.3) | copy-done | bytes 88
  3.1 50.0 %packed_attention.1 = bf16[128,1024]{1,0:T(8,128)(2,1)S(1)} custom-call(bf16[128,1024]{1,0:T(8,128)(2,1)S(1)} %copy-done, bf16[128,128]{1,0:T(8,128)(2,1)S(1)} %copy-done.1, bf16[128,128]{1,0:T(8,128)(2,1)S(1)} %copy-done.2, s32[16]{0:T(128)S(1)} %copy-done.3), custom_call_target="tpu_custom_call" | custom-call | tf_op jit(solution)/shard_map/packed_attention/pallas_call | solution.py:356
  53.2 0.7 %copy.6 = bf16[128,1024]{1,0:T(8,128)(2,1)} copy(bf16[128,1024]{1,0:T(8,128)(2,1)S(1)} %packed_attention.1) | data formatting | bytes 524288
Async XLA Ops:
  0.0 0.9 %copy-start = (bf16[128,1024]{1,0:T(8,128)(2,1)S(1)}, bf16[128,1024]{1,0:T(8,128)(2,1)}, u32[]{:S(2)}) copy-start(bf16[128,1024]{1,0:T(8,128)(2,1)} %q_ref.1) | copy-start | bytes 786436
  1.0 0.8 %copy-start.1 = (bf16[128,128]{1,0:T(8,128)(2,1)S(1)}, bf16[128,128]{1,0:T(8,128)(2,1)}, u32[]{:S(2)}) copy-start(bf16[128,128]{1,0:T(8,128)(2,1)} %k_ref.1) | copy-start | bytes 98308
  1.7 0.8 %copy-start.2 = (bf16[128,128]{1,0:T(8,128)(2,1)S(1)}, bf16[128,128]{1,0:T(8,128)(2,1)}, u32[]{:S(2)}) copy-start(bf16[128,128]{1,0:T(8,128)(2,1)} %v_ref.1) | copy-start | bytes 98308
  2.5 0.7 %copy-start.3 = (s32[16]{0:T(128)S(1)}, s32[16]{0:T(128)}, u32[]{:S(2)}) copy-start(s32[16]{0:T(128)} %len_ref.1) | copy-start | bytes 196
